TPU v7x, 32 devices: a whole 2x2x4 slice. The times are simulated.
32 devices in a mesh: seg: 4 (over y, core), band: 8 (over z, x).
Axes of the slice: x: 2, y: 2, z: 4, core: 2. Of those that a mesh axis runs over, the one named last changes fastest.
Arguments:
- sft: bfloat16 [8, 2, 2, 2048], P('seg', None, None, 'band'), may hold values from -6 to 6
- doppler: float32 [8, 512], P('seg'), may hold values from -16 to 16
- antenna: float32 [8, 2, 2, 512], P('seg'), may hold values from -1 to 1
- coarse_index: int32 [8, 128], P('seg'), may hold values from 0 to 511
- freq_offset: int32 [8, 128], P('seg'), may hold values from -32 to 32
- wing_width: int32 [8], replicated, may hold values from 8 to 32
Outputs:
- fstat: float32 [128, 2048], P('seg', 'band')
All inputs are finite; a program needn't handle non-finite values.
Results may differ from a plain program's by a relative error of at most 0.00088.
Values may be sent and summed in bfloat16 or wider, within the bound.
A program may use at most 64 MiB of HBM per device.

v0:
```python
import math

import jax
import jax.numpy as jnp
from jax import lax
from jax.sharding import PartitionSpec as P

WMAX = 32
OMAX = 32


def with_halo(block, sides, width):
    for axis, dim in sides:
        count = lax.axis_size(axis)
        forward = [(i, i + 1) for i in range(count - 1)]
        backward = [(target, source) for source, target in forward]
        low = lax.ppermute(
            lax.slice_in_dim(block, block.shape[dim] - width, None, axis=dim), axis, forward
        )
        high = lax.ppermute(lax.slice_in_dim(block, 0, width, axis=dim), axis, backward)
        block = jnp.concatenate([low, block, high], axis=dim)
    return block


def kernel_block(shifts, weights):
    tap_pos = jnp.arange(2 * WMAX).astype(jnp.float32) - WMAX
    offsets = tap_pos[None, None, :] - shifts[:, :, None]
    envelope = jnp.sinc(offsets)
    real_part = envelope * jnp.cos(jnp.pi * offsets)
    imag_part = -envelope * jnp.sin(jnp.pi * offsets)
    from_real = jnp.stack([real_part, imag_part], -1)
    from_imag = jnp.stack([-imag_part, real_part], -1)
    stacked = jnp.transpose(jnp.stack([from_real, from_imag], 1), (0, 1, 3, 2, 4))
    antenna_t = jnp.transpose(weights, (0, 2, 3, 1))
    product = antenna_t[:, :, None, None, :, :, None] * stacked[:, None, :, :, :, None, :]
    count_seg = shifts.shape[0]
    return product.astype(jnp.bfloat16).reshape(count_seg, -1, shifts.shape[1] * 4)


def coarse_stat(padded, doppler, antenna, wing_width, first_bin, bin_count, band_bins):
    segs_here = padded.shape[0]
    tap_count = 2 * WMAX
    unfolded = jnp.stack(
        [padded[:, :, :, column : column + bin_count] for column in range(tap_count)], axis=3
    )
    global_bin = first_bin + jnp.arange(bin_count)
    subband = global_bin // band_bins
    member = subband[:, None] == jnp.arange(wing_width.shape[0])[None, :]
    wing_reach = jnp.sum(jnp.where(member, wing_width[None, :], 0), axis=1)
    tap_index = jnp.arange(tap_count) - WMAX
    inside = (tap_index[:, None] >= -wing_reach[None, :]) & (
        tap_index[:, None] < wing_reach[None, :]
    )
    unfolded = unfolded * inside.astype(jnp.bfloat16)
    unfolded = unfolded.reshape(segs_here, -1, bin_count)
    coarse_count = doppler.shape[1]
    block_size = math.gcd(coarse_count, 256 >> min(3, (segs_here // 4).bit_length()))
    blocks = coarse_count // block_size
    shift_blocks = jnp.moveaxis(doppler.reshape(segs_here, blocks, block_size), 1, 0)
    weight_blocks = jnp.moveaxis(
        antenna.reshape(segs_here, 2, antenna.shape[2], blocks, block_size), 3, 0
    )

    def one_block(block_args):
        kernel = kernel_block(block_args[0], block_args[1])
        amplitude = jnp.einsum("skf,skn->snf", unfolded, kernel, preferred_element_type=jnp.float32)
        amplitude = amplitude.reshape(segs_here, block_size, 4, bin_count)
        return 0.25 * jnp.sum(amplitude * amplitude, axis=2)

    result = lax.map(one_block, (shift_blocks, weight_blocks))
    return jnp.transpose(result, (1, 0, 2, 3)).reshape(segs_here, coarse_count, bin_count)


def fine_sums(coarse, coarse_index, freq_offset, width):
    window = jax.vmap(
        lambda row_data, shift_bins: lax.dynamic_slice_in_dim(row_data, shift_bins + OMAX, width)
    )

    def add_segment(partial_sum, inputs):
        segment_coarse, indices, offsets = inputs
        picked = jnp.take(segment_coarse, indices, axis=0)
        return (partial_sum + window(picked, offsets), None)

    initial = jnp.zeros((coarse_index.shape[1], width), jnp.float32)
    total, unused = lax.scan(add_segment, initial, (coarse, coarse_index, freq_offset))
    return total


def per_device(sft, doppler, antenna, coarse_index, freq_offset, wing_width):
    band_bins = sft.shape[3]
    band_start = lax.axis_index("band") * band_bins
    seg_count = lax.axis_size("seg")
    total_segments = sft.shape[0] * seg_count
    padded = with_halo(sft, (("band", 3),), WMAX + OMAX)
    coarse = coarse_stat(
        padded, doppler, antenna, wing_width, band_start - OMAX, band_bins + 2 * OMAX, band_bins
    )
    partial_sum = fine_sums(coarse, coarse_index, freq_offset, band_bins)
    summed = lax.psum_scatter(partial_sum, "seg", scatter_dimension=0, tiled=True)
    return summed * (1.0 / total_segments)


def solution(mesh):
    placed = (
        P("seg", None, None, "band"),
        P("seg", None),
        P("seg", None, None, None),
        P("seg", None),
        P("seg", None),
        P(),
    )
    return jax.shard_map(
        per_device, mesh=mesh, in_specs=placed, out_specs=P("seg", "band"), check_vma=False
    )
```

profile of v0, /device:TPU:0, one launch (start us, length us, event | category | flops | bytes accessed | tf_op | source)
XLA Modules:
  0.0 628.0 jit_solution(7149569180443043950)
XLA Ops:
  7.3 4.8 collective-permute-start
  15.9 1.8 collective-permute-done.1
  24.3 35.5 %while.32 = (s32[]{:T(128)}, f32[2,2,256,320]{3,1,2,0:T(2,128)}, f32[2,2,2,2,256]{4,0,3,2,1:T(2,128)S(1)}, f32[2,2,256]{2,1,0:T(2,128)S(1)}, bf16[2,256,320]{1,2,0:T(8,128)(2,1)S(1)}) while((s32[]{:T(128)}, f32[2,2,256,320]{3,1,2,0:T(2,128)}, f32[2,2,2,2,256]{4,0,3,2,1:T(2,128)S(1)}, f32[2,2,256]{2,1,0:T(2,128)S(1)}, ...), condition=%wide.region_3.4_spmd.clone, body=%wide.region_1.3_spmd.sunk.clone | while | flops 339443840 | bytes 21085252 | solution.py:70
  26.9 4.3 multiply_convert_fusion.3
  32.6 2.1 convolution_multiply_fusion.3
  34.6 4.5 copy.48
  39.1 1.6 bitcast_reduce_fusion.3
  44.6 4.3 multiply_convert_fusion.3
  50.3 2.1 convolution_multiply_fusion.3
  52.4 4.5 copy.48
  56.9 1.6 bitcast_reduce_fusion.3
  59.7 1.5 copy.37
  61.3 536.8 %while.34 = (s32[]{:T(128)}, f32[128,256]{1,0:T(8,128)S(1)}, s32[2,128]{1,0:T(2,128)S(1)}, f32[2,512,320]{2,1,0:T(8,128)S(1)}, s32[2,128]{1,0:T(2,128)S(1)}, /*index=5*/s32[]{:T(128)}, s32[]{:T(128)}, f32[]{:T(128)}) while((s32[]{:T(128)}, f32[128,256]{1,0:T(8,128)S(1)}, s32[2,128]{1,0:T(2,128)S(1)}, ...), condition=%wide.region_5.6_spmd.clone.clone, body=%wide.region_4.5_spmd.clone.sunk.clone | while | flops 109445 | bytes 2374168 | solution.py:85
  62.4 267.3 %while.33 = (s32[]{:T(128)}, f32[128,320]{1,0:T(8,128)S(1)}, s32[128,2]{0,1:T(2,128)S(1)}, f32[128,256]{1,0:T(8,128)S(1)}, s32[]{:T(128)}, /*index=5*/s32[]{:T(128)}) while((s32[]{:T(128)}, f32[128,320]{1,0:T(8,128)S(1)}, s32[128,2]{0,1:T(2,128)S(1)}, f32[128,256]{1,0:T(8,128)S(1)}, s32[]{:T(128)}, /*index=5*/s32[]{:T(128)}) %tuple.91), condition=%wide.while_cond, body=%wide.while_body.sunk | while | flops 2 | bytes 4209 | solution.py:76
  81.8 1.4 dynamic-slice.7
  83.9 1.4 dynamic-slice.7
  86.0 1.4 dynamic-slice.7
  88.1 1.4 dynamic-slice.7
  121.5 1.4 dynamic-slice.7
  123.6 1.4 dynamic-slice.7
  125.7 1.4 dynamic-slice.7
  127.8 1.4 dynamic-slice.7
  161.2 1.4 dynamic-slice.7
  163.3 1.4 dynamic-slice.7
  165.4 1.4 dynamic-slice.7
  167.4 1.4 dynamic-slice.7
  200.9 1.4 dynamic-slice.7
  203.0 1.4 dynamic-slice.7
  205.0 1.4 dynamic-slice.7
  207.1 1.4 dynamic-slice.7
  240.5 1.4 dynamic-slice.7
  242.6 1.4 dynamic-slice.7
  244.7 1.4 dynamic-slice.7
  246.8 1.4 dynamic-slice.7
  280.2 1.4 dynamic-slice.7
  282.3 1.4 dynamic-slice.7
  284.4 1.4 dynamic-slice.7
  286.5 1.4 dynamic-slice.7
  319.9 1.4 dynamic-slice.7
  322.0 1.4 dynamic-slice.7
  324.1 1.4 dynamic-slice.7
  326.2 1.4 dynamic-slice.7
  330.8 267.3 %while.33 = (s32[]{:T(128)}, f32[128,320]{1,0:T(8,128)S(1)}, s32[128,2]{0,1:T(2,128)S(1)}, f32[128,256]{1,0:T(8,128)S(1)}, s32[]{:T(128)}, /*index=5*/s32[]{:T(128)}) while((s32[]{:T(128)}, f32[128,320]{1,0:T(8,128)S(1)}, s32[128,2]{0,1:T(2,128)S(1)}, f32[128,256]{1,0:T(8,128)S(1)}, s32[]{:T(128)}, /*index=5*/s32[]{:T(128)}) %tuple.91), condition=%wide.while_cond, body=%wide.while_body.sunk | while | flops 2 | bytes 4209 | solution.py:76
  348.2 1.4 dynamic-slice.7
  350.2 1.4 dynamic-slice.7
  352.3 1.4 dynamic-slice.7
  354.4 1.4 dynamic-slice.7
  598.8 20.9 %reduce-scatter.2.cloned.1.call-done = f32[32,256]{1,0:T(8,128)} async-done(((f32[128,256]{1,0:T(8,128)}), f32[32,256]{1,0:T(8,128)}) %reduce-scatter.2.cloned.1.call-update) | async-done | bytes 32784 | tf_op jit(solution)/shard_map/reduce_scatter | solution.py:99
  (1127 shorter events, 511.4 us)
Async XLA Ops:
  6.5 17.7 %copy-start.2 = (f32[2,512]{1,0:T(2,128)S(1)}, f32[2,512]{1,0:T(2,128)}, u32[]{:S(2)}) copy-start(f32[2,512]{1,0:T(2,128)} %param.11) | copy-start | bytes 12292
  6.5 613.2 %reduce-scatter.2.cloned.1.call-start = ((), (), s32[]{:S(2)}) async-start(), calls=%async_computation.1 | async-start | bytes 163840 | tf_op jit(solution)/shard_map/reduce_scatter | solution.py:99
  7.3 7.8 %collective-permute-start = (bf16[2,2,2,64]{3,2,1,0:T(2,128)(2,1)S(1)}, bf16[2,2,2,64]{3,2,1,0:T(2,128)(2,1)S(1)}, u32[]{:S(2)}, u32[]{:S(2)}) collective-permute-start(bf16[2,2,2,64]{3,2,1,0:T(2,128)(2,1)S(1)} %get-tuple-element.222), channel_id=1, source_target_pairs={{0,1},{1,2},{2,3},{3,4},{4,5},{5,6},{6,7},{8,9},{9,10},{10,11},{11... | collective-permute-start | bytes 3080 | tf_op jit(solution)/shard_map/ppermute | solution.py:17
  12.2 5.5 collective-permute-start.1
  59.7 1.6 copy-start
  59.7 1.6 copy-start.3
  59.7 1.6 copy-start.4
  598.2 0.7 copy-start.1
Sparse Core Ops, SparseCore 0:
  598.9 20.7 reduce-scatter.1
where the time goes:
time: 633 us; the launch traced here: 628 us
  local copies, waits for them, and re-layouts  557 us (88%)
  waiting for transfers between devices  22.7 us (4%)
  other arithmetic  20.1 us (3%)
  between operations  13.7 us (2%)
    gather x1024, local copies, waits for them, and re-layouts  530 us
    reduce_scatter x1, waiting for transfers between devices, per_device(): lax.psum_scatter(partial_sum, 'seg', scatter_dimension=0, tiled=True)  20.9 us
  transfers between devices with their start and end apart: 3, of which 2 were waited for; matrix products, arithmetic and copies ran while one was open for 0% of the time, Pallas kernels for 0%

commit v1 on v0

v1 whole, which is shorter than its diff:
```python
import functools
import math

import jax
import jax.numpy as jnp
from jax import lax
from jax.experimental import pallas as pl
from jax.experimental.pallas import tpu as pltpu
from jax.sharding import PartitionSpec as P

WMAX = 32
OMAX = 32
TAPS = 2 * WMAX
LANES = 128
ROWS = 8
MESH = pl.DeviceIdType.MESH


def half_turn(x):
    rest = x - jnp.round(x)
    angle = rest * math.pi
    square = angle * angle
    sine = jnp.zeros_like(x)
    cosine = jnp.zeros_like(x)
    for power in range(7, -1, -1):
        sign = -1.0 if power % 2 else 1.0
        cosine = cosine * square + sign / math.factorial(2 * power)
        sine = sine * square + sign / math.factorial(2 * power + 1)
    return sine * angle, cosine


def gathered_rows(rows, indices):
    first = rows.astype(jnp.bfloat16).astype(jnp.float32)
    rest = rows - first
    second = rest.astype(jnp.bfloat16).astype(jnp.float32)
    third = rest - second
    parts = jnp.concatenate([first, second, third, jnp.zeros_like(first)], axis=0)
    places = lax.broadcasted_iota(jnp.int32, (rows.shape[1], indices.shape[1]), 0)
    chosen = jnp.where(places == indices, 1.0, 0.0).astype(jnp.bfloat16)
    picked = jnp.dot(parts.astype(jnp.bfloat16), chosen, preferred_element_type=jnp.float32)
    count = rows.shape[0]
    return picked[:count] + picked[count : 2 * count] + picked[2 * count : 3 * count]


def kernel(
    n_seg,
    n_band,
    scale,
    sft_ref,
    doppler_ref,
    antenna_ref,
    index_ref,
    offset_ref,
    wing_ref,
    out_ref,
    x_ref,
    edge_ref,
    param_ref,
    fine_ref,
    part_ref,
    recv_ref,
    edge_send,
    edge_recv,
    part_send,
    part_recv,
):
    seg = lax.axis_index("seg")
    band = lax.axis_index("band")
    segs_here, dets, _, bins = sft_ref.shape
    fine = index_ref.shape[1]
    own = fine // n_seg
    lines = 2 * dets
    up = lax.rem(band + 1, n_band)
    down = lax.rem(band + n_band - 1, n_band)

    barrier = pltpu.get_barrier_semaphore()
    for neighbour in (up, down):
        pl.semaphore_signal(barrier, inc=1, device_id={"band": neighbour}, device_id_type=MESH)
    for step in range(1, n_seg):
        pl.semaphore_signal(
            barrier,
            inc=1,
            device_id={"seg": lax.rem(seg + step, n_seg)},
            device_id_type=MESH,
        )

    for s in range(segs_here):
        for d in range(dets):
            first = s * lines + 2 * d
            x_ref[first : first + 2, :] = sft_ref[s, d].astype(jnp.float32)
    pl.semaphore_wait(barrier, n_seg + 1)

    edges = []
    for side, (neighbour, start) in enumerate(((up, bins - LANES), (down, 0))):
        edges.append(
            pltpu.make_async_remote_copy(
                src_ref=x_ref.at[:, pl.ds(start, LANES)],
                dst_ref=edge_ref.at[side],
                send_sem=edge_send.at[side],
                recv_sem=edge_recv.at[side],
                device_id={"band": neighbour},
                device_id_type=MESH,
            )
        )
        edges[-1].start()

    param_ref[...] = jnp.zeros_like(param_ref)
    fine_ref[...] = jnp.zeros_like(fine_ref)
    for s in range(segs_here):
        param_ref[ROWS * s : ROWS * s + 1, :] = doppler_ref[s : s + 1, :]
        for q in range(2):
            first = ROWS * s + 1 + dets * q
            param_ref[first : first + dets, :] = antenna_ref[s, q]
    for s in range(segs_here):
        rows = gathered_rows(param_ref[ROWS * s : ROWS * (s + 1), :], index_ref[s : s + 1, :])
        fine_ref[ROWS * s : ROWS * (s + 1), :] = rows
        sine, cosine = half_turn(rows[0:1])
        fine_ref[ROWS * s + 5 : ROWS * s + 6, :] = offset_ref[s : s + 1, :].astype(jnp.float32)
        fine_ref[ROWS * s + 6 : ROWS * s + 7, :] = sine
        fine_ref[ROWS * s + 7 : ROWS * s + 8, :] = cosine
    columns = jnp.transpose(fine_ref[...])

    lane = lax.broadcasted_iota(jnp.int32, (fine, 2 * TAPS), 1)
    from_real = lane < TAPS
    tap = (WMAX - 1 - lax.rem(lane, TAPS)).astype(jnp.float32)
    kernels = []
    for s in range(segs_here):
        column = lambda row: columns[:, ROWS * s + row : ROWS * s + row + 1]
        u = tap - column(0)
        centre = u == 0.0
        envelope = jnp.where(
            centre, 1.0, -column(6) / jnp.where(centre, 1.0, math.pi * u)
        )
        real_part = envelope * column(7)
        imag_part = envelope * column(6)
        to_real = jnp.where(from_real, real_part, -imag_part)
        to_imag = jnp.where(from_real, imag_part, real_part)
        blocks = []
        for q in range(2):
            for shape in (to_real, to_imag):
                pieces = [column(1 + dets * q + d) * shape for d in range(dets)]
                blocks.append(jnp.concatenate(pieces, axis=1))
        kernels.append(jnp.concatenate(blocks, axis=0).astype(jnp.bfloat16))

    width = bins + 2 * (WMAX + OMAX)
    wing_low = jnp.where(band > 0, wing_ref[jnp.maximum(band - 1, 0)], 0)
    wing_mid = wing_ref[band]
    wing_high = jnp.where(band < n_band - 1, wing_ref[jnp.minimum(band + 1, n_band - 1)], 0)
    position = lax.broadcasted_iota(jnp.int32, (TAPS, width), 1)
    reach = jnp.where(
        position < OMAX, wing_low, jnp.where(position < OMAX + bins, wing_mid, wing_high)
    )
    tap_here = WMAX - 1 - lax.broadcasted_iota(jnp.int32, (TAPS, width), 0)
    inside = (tap_here >= -reach) & (tap_here < reach)

    for edge in edges:
        edge.wait()
    low = jnp.where(band > 0, edge_ref[0], 0.0)
    high = jnp.where(band < n_band - 1, edge_ref[1], 0.0)
    padded = jnp.concatenate([low, x_ref[...], high], axis=1)
    margin = LANES - WMAX - OMAX
    padded = pltpu.roll(padded, padded.shape[1] - margin, 1)[:, :width]

    total = None
    for s in range(segs_here):
        unfolded = []
        for line in range(s * lines, (s + 1) * lines):
            spread = jnp.broadcast_to(padded[line : line + 1, :], (TAPS, width))
            spread = pltpu.roll(spread, width - TAPS + 1, 1, stride=1, stride_axis=0)
            unfolded.append(jnp.where(inside, spread, 0.0))
        unfolded = jnp.concatenate(unfolded, axis=0).astype(jnp.bfloat16)
        amplitude = jnp.dot(kernels[s], unfolded, preferred_element_type=jnp.float32)
        power = amplitude * amplitude
        coarse = (power[:fine] + power[fine : 2 * fine]) + (
            power[2 * fine : 3 * fine] + power[3 * fine :]
        )
        shift = columns[:, ROWS * s + 5 : ROWS * s + 6].astype(jnp.int32) + OMAX
        for bit in range((2 * OMAX).bit_length()):
            moved = pltpu.roll(coarse, width - (1 << bit), 1)
            coarse = jnp.where((shift & (1 << bit)) != 0, moved, coarse)
        total = coarse[:, :bins] if total is None else total + coarse[:, :bins]
    part_ref[...] = total * scale

    sends = []
    for step in range(1, n_seg):
        peer = lax.rem(seg + step, n_seg)
        sends.append(
            pltpu.make_async_remote_copy(
                src_ref=part_ref.at[pl.ds(pl.multiple_of(peer * own, own), own)],
                dst_ref=recv_ref.at[step - 1],
                send_sem=part_send.at[step - 1],
                recv_sem=part_recv.at[step - 1],
                device_id={"seg": peer},
                device_id_type=MESH,
            )
        )
        sends[-1].start()
    result = part_ref[pl.ds(pl.multiple_of(seg * own, own), own), :]
    for step in range(1, n_seg):
        sends[step - 1].wait_recv()
        result = result + recv_ref[step - 1]
    out_ref[...] = result
    for send in sends:
        send.wait_send()


def solution(mesh):
    n_seg = mesh.shape["seg"]
    n_band = mesh.shape["band"]
    placed = (
        P("seg", None, None, "band"),
        P("seg", None),
        P("seg", None, None, None),
        P("seg", None),
        P("seg", None),
        P(),
    )

    def per_device(sft, doppler, antenna, coarse_index, freq_offset, wing_width):
        segs_here, dets, _, bins = sft.shape
        fine = coarse_index.shape[1]
        own = fine // n_seg
        lines = segs_here * dets * 2
        vmem = pl.BlockSpec(memory_space=pltpu.VMEM)
        smem = pl.BlockSpec(memory_space=pltpu.SMEM)
        return pl.pallas_call(
            functools.partial(kernel, n_seg, n_band, 0.25 / (segs_here * n_seg)),
            out_shape=jax.ShapeDtypeStruct((own, bins), jnp.float32),
            in_specs=[vmem] * 5 + [smem],
            out_specs=vmem,
            scratch_shapes=[
                pltpu.VMEM((lines, bins), jnp.float32),
                pltpu.VMEM((2, lines, LANES), jnp.float32),
                pltpu.VMEM((ROWS * segs_here, doppler.shape[1]), jnp.float32),
                pltpu.VMEM((LANES, fine), jnp.float32),
                pltpu.VMEM((fine, bins), jnp.float32),
                pltpu.VMEM((n_seg - 1, own, bins), jnp.float32),
                pltpu.SemaphoreType.DMA((2,)),
                pltpu.SemaphoreType.DMA((2,)),
                pltpu.SemaphoreType.DMA((n_seg - 1,)),
                pltpu.SemaphoreType.DMA((n_seg - 1,)),
            ],
            compiler_params=pltpu.CompilerParams(
                collective_id=0, has_side_effects=True, vmem_limit_bytes=40 * 1024 * 1024
            ),
        )(sft, doppler, antenna, coarse_index, freq_offset, wing_width)

    return jax.shard_map(
        per_device, mesh=mesh, in_specs=placed, out_specs=P("seg", "band"), check_vma=False
    )
```

time: 633 us -> 18.8 us (0.03)
  local copies, waits for them, and re-layouts: 557 us -> 4.72 us
  waiting for transfers between devices: 22.7 us -> 0 us
  other arithmetic: 20.1 us -> 0 us
  Pallas kernels: 0 us -> 13.7 us
  between operations: 13.7 us -> 0.02 us
    gather x1026 -> x0, local copies, waits for them, and re-layouts: 532 us -> none
    reduce_scatter x1 -> x0, waiting for transfers between devices: 20.9 us -> none  [per_device(): lax.psum_scatter(partial_sum, 'seg', scatter_dimension=0, tiled=True)]
    pallas_call x0 -> x1, Pallas kernels: none -> 13.7 us  [per_device(): pl.pallas_call(functools.partial(kernel, n_seg, n_band, 0.25 / (segs_here...]
    mul x3 -> x0, local copies, waits for them, and re-layouts: 9.01 us -> none  [the longest x2 8.99 us: one_block(): return 0.25 * jnp.sum(amplitude * amplitude, axis=2)]
    convert_element_type x3 -> x0, other arithmetic: 8.71 us -> none  [the longest x2 8.63 us: kernel_block(): product.astype(jnp.bfloat16).reshape(count_seg, -1, shifts.shape[1] * 4)]
  transfers between devices with their start and end apart: 3 -> 0, of which waited for: 2 -> 0; matrix products, arithmetic and copies ran while one was open for 0% -> 0% of each run, Pallas kernels for 0% -> 0%
where the time goes in v1:
time: 18.8 us; the launch traced here: 18.4 us
  Pallas kernels  13.7 us (73%)
  local copies, waits for them, and re-layouts  4.72 us (25%)
    pallas_call x1, Pallas kernels, per_device(): pl.pallas_call(functools.partial(kernel, n_seg, n_band, 0.25 / (segs_here...  13.7 us
    unnamed x13, local copies, waits for them, and re-layouts  4.72 us

profile of v1, /device:TPU:0, one launch (start us, length us, event | category | flops | bytes accessed | tf_op | source)
XLA Modules:
  0.0 18.4 jit_solution(3427809489620395119)
XLA Ops:
  0.0 0.0 copy-start
  0.0 0.7 %copy-done = f32[2,2,2,512]{3,2,1,0:T(2,128)S(1)} copy-done((f32[2,2,2,512]{3,2,1,0:T(2,128)S(1)}, f32[2,2,2,512]{3,2,1,0:T(2,128)}, u32[]{:S(2)}) %copy-start) | copy-done | bytes 16408
  0.7 0.0 copy-start.1
  0.7 0.7 %copy-done.1 = bf16[2,2,2,256]{3,2,1,0:T(2,128)(2,1)S(1)} copy-done((bf16[2,2,2,256]{3,2,1,0:T(2,128)(2,1)S(1)}, bf16[2,2,2,256]{3,2,1,0:T(2,128)(2,1)}, u32[]{:S(2)}) %copy-start.1) | copy-done | bytes 4120
  1.4 0.0 copy-start.2
  1.4 0.7 %copy-done.2 = f32[2,512]{1,0:T(2,128)S(1)} copy-done((f32[2,512]{1,0:T(2,128)S(1)}, f32[2,512]{1,0:T(2,128)}, u32[]{:S(2)}) %copy-start.2) | copy-done | bytes 4120
  2.1 0.0 copy-start.3
  2.1 0.7 %copy-done.3 = s32[2,128]{1,0:T(2,128)S(1)} copy-done((s32[2,128]{1,0:T(2,128)S(1)}, s32[2,128]{1,0:T(2,128)}, u32[]{:S(2)}) %copy-start.3) | copy-done | bytes 1048
  2.8 0.0 copy-start.4
  2.8 0.7 %copy-done.4 = s32[2,128]{1,0:T(2,128)S(1)} copy-done((s32[2,128]{1,0:T(2,128)S(1)}, s32[2,128]{1,0:T(2,128)}, u32[]{:S(2)}) %copy-start.4) | copy-done | bytes 1048
  3.5 0.0 copy-start.5
  3.5 0.7 %copy-done.5 = s32[8]{0:T(128)S(1)} copy-done((s32[8]{0:T(128)S(1)}, s32[8]{0:T(128)}, u32[]{:S(2)}) %copy-start.5) | copy-done | bytes 56
  4.1 13.7 %shard_map.64 = f32[32,256]{1,0:T(8,128)S(1)} custom-call(bf16[2,2,2,256]{3,2,1,0:T(2,128)(2,1)S(1)} %copy-done.1, f32[2,512]{1,0:T(2,128)S(1)} %copy-done.2, f32[2,2,2,512]{3,2,1,0:T(2,128)S(1)} %copy-done, s32[2,128]{1,0:T(2,128)S(1)} %copy-done.3, s32[2,128]{1,0:T(2,128)S(1)} %copy-done.4, s32[8]{0:T(128)S(1)} %copy-done.5), custom_call_target="tpu_custom_call" | custom-call | tf_op jit(solution)/shard_map/pallas_call | solution.py:226
  17.8 0.6 %copy.8 = f32[32,256]{1,0:T(8,128)} copy(f32[32,256]{1,0:T(8,128)S(1)} %shard_map.64) | data formatting | bytes 65536
Async XLA Ops:
  0.0 0.7 %copy-start = (f32[2,2,2,512]{3,2,1,0:T(2,128)S(1)}, f32[2,2,2,512]{3,2,1,0:T(2,128)}, u32[]{:S(2)}) copy-start(f32[2,2,2,512]{3,2,1,0:T(2,128)} %antenna_ref.1) | copy-start | bytes 49156
  0.7 0.7 %copy-start.1 = (bf16[2,2,2,256]{3,2,1,0:T(2,128)(2,1)S(1)}, bf16[2,2,2,256]{3,2,1,0:T(2,128)(2,1)}, u32[]{:S(2)}) copy-start(bf16[2,2,2,256]{3,2,1,0:T(2,128)(2,1)} %sft_ref.1) | copy-start | bytes 12292
  1.4 0.7 %copy-start.2 = (f32[2,512]{1,0:T(2,128)S(1)}, f32[2,512]{1,0:T(2,128)}, u32[]{:S(2)}) copy-start(f32[2,512]{1,0:T(2,128)} %doppler_ref.1) | copy-start | bytes 12292
  2.1 0.7 %copy-start.3 = (s32[2,128]{1,0:T(2,128)S(1)}, s32[2,128]{1,0:T(2,128)}, u32[]{:S(2)}) copy-start(s32[2,128]{1,0:T(2,128)} %index_ref.1) | copy-start | bytes 3076
  2.8 0.7 %copy-start.4 = (s32[2,128]{1,0:T(2,128)S(1)}, s32[2,128]{1,0:T(2,128)}, u32[]{:S(2)}) copy-start(s32[2,128]{1,0:T(2,128)} %offset_ref.1) | copy-start | bytes 3076
  3.5 0.7 %copy-start.5 = (s32[8]{0:T(128)S(1)}, s32[8]{0:T(128)}, u32[]{:S(2)}) copy-start(s32[8]{0:T(128)} %wing_ref.1) | copy-start | bytes 100
